TPU v7x, 32 devices: a whole 2x2x4 slice. The times are simulated.
32 devices in a mesh: grp: 2 (over x), loop: 16 (over z, y, core).
Axes of the slice: x: 2, y: 2, z: 4, core: 2. Of those that a mesh axis runs over, the one named last changes fastest.
Arguments:
- hidden: bfloat16 [2, 256, 14848], P(None, ('grp', 'loop')), parts along dimension 1, may hold values from -6 to 6
- lengths: int32 [256], P(('grp', 'loop')), parts along dimension 0, may hold values from 1 to 256, as said below
- cache_keys: bfloat16 [256, 256, 64], P(('grp', 'loop')), parts along dimension 0, may hold values from -600 to 600
- cache_values: bfloat16 [256, 256, 64], P(('grp', 'loop')), parts along dimension 0, may hold values from -6 to 6
- ln_gain: float32 [14848], replicated, may hold values from 0.5 to 1.5
- ln_bias: float32 [14848], replicated, may hold values from -3 to 3
- w_qkv: bfloat16 [14848, 1984], P('loop'), may hold values from -0.046875 to 0.046875
- w_out: bfloat16 [1856, 14848], P(None, 'loop'), may hold values from -0.125 to 0.125
Outputs:
- results: bfloat16 [2, 256, 14848], P(None, ('grp', 'loop')), parts along dimension 1
There are 2 independent parts, one for each index of `grp`. A program takes and returns all parts, laid end to end along the dimension named above; an argument that names none is the same for every part. Nothing has to cross between parts.
Inputs may be any that keep to these rules, and one draw needn't show every extreme that they name: `lengths`: every row has at least one filled position; some row of every draw has all 256 filled and some row has one.
All inputs are finite; a program needn't handle non-finite values.
Results may differ from a plain program's by a relative error of at most 0.012.
Values may be sent and summed in bfloat16 or wider, within the bound.
A program may use at most 64 MiB of HBM per device.

v0:
```python
import jax
import jax.numpy as jnp
from jax import lax
from jax.sharding import PartitionSpec as P


def layer_norm(current, ln_gain, ln_bias):
    values = current.astype(jnp.float32)
    average = jnp.mean(values, axis=-1, keepdims=True)
    centred = values - average
    variance = jnp.mean(centred * centred, axis=-1, keepdims=True)
    return (centred * lax.rsqrt(variance + 1e-05) * ln_gain + ln_bias).astype(jnp.bfloat16)


def attend(queries, all_keys, all_values, visible):
    scores = (
        jnp.einsum("rhe,rpe->rhp", queries, all_keys, preferred_element_type=jnp.float32) * 0.125
    )
    scores = jnp.where(visible[:, None, :], scores, -1e30)
    maxima = jnp.max(scores, axis=-1, keepdims=True)
    exps = jnp.where(visible[:, None, :], jnp.exp(scores - maxima), 0.0)
    totals = jnp.sum(exps, axis=-1, keepdims=True)
    probs = (exps / totals).astype(jnp.bfloat16)
    mixed = jnp.einsum("rhp,rpe->rhe", probs, all_values, preferred_element_type=jnp.float32)
    return mixed.reshape(mixed.shape[0], -1).astype(jnp.bfloat16)


def local(hidden, lengths, cache_keys, cache_values, ln_gain, ln_bias, w_qkv, w_out):
    step_count = hidden.shape[0]
    local_rows = hidden.shape[1]
    context = cache_keys.shape[1]
    head_dim = cache_keys.shape[2]
    width = w_qkv.shape[1]
    heads_count = width // head_dim - 2
    visible_cache = jnp.arange(context, dtype=jnp.int32)[None, :] < lengths[:, None]
    normed_list = [
        layer_norm(hidden[step_index], ln_gain, ln_bias) for step_index in range(step_count)
    ]
    projections = []
    for step_index in range(step_count):
        spread_one = lax.all_to_all(
            normed_list[step_index], "loop", split_axis=1, concat_axis=0, tiled=True
        )

        def one_term(start, count, source=spread_one):
            return jnp.dot(source, w_qkv, preferred_element_type=jnp.float32)

        projections.append(
            lax.psum_scatter(
                one_term(jnp.int32(0), local_rows * lax.axis_size("loop")),
                "loop",
                scatter_dimension=0,
                tiled=True,
            ).astype(jnp.bfloat16)
        )
    fresh_keys = []
    fresh_values = []
    results = []
    for step_index in range(step_count):
        current = hidden[step_index]
        projected = projections[step_index]
        queries = projected[:, : heads_count * head_dim].reshape(local_rows, heads_count, head_dim)
        fresh_keys.append(projected[:, heads_count * head_dim : (heads_count + 1) * head_dim])
        fresh_values.append(projected[:, (heads_count + 1) * head_dim :])
        all_keys = jnp.concatenate([cache_keys, jnp.stack(fresh_keys, 1)], 1)
        all_values = jnp.concatenate([cache_values, jnp.stack(fresh_values, 1)], 1)
        visible = jnp.concatenate([visible_cache, jnp.ones((local_rows, step_index + 1), bool)], 1)
        mixed_heads = attend(queries, all_keys, all_values, visible)
        every_row = lax.all_gather(mixed_heads, "loop", axis=0, tiled=True)
        columns_out = jnp.dot(every_row, w_out, preferred_element_type=jnp.float32).astype(
            jnp.bfloat16
        )
        attention = lax.all_to_all(columns_out, "loop", split_axis=0, concat_axis=1, tiled=True)
        results.append(
            (current.astype(jnp.float32) + attention.astype(jnp.float32)).astype(jnp.bfloat16)
        )
    return jnp.stack(results)


def solution(mesh):
    return jax.shard_map(
        local,
        mesh=mesh,
        in_specs=(
            P(None, ("grp", "loop"), None),
            P(("grp", "loop")),
            P(("grp", "loop"), None, None),
            P(("grp", "loop"), None, None),
            P(),
            P(),
            P("loop", None),
            P(None, "loop"),
        ),
        out_specs=P(None, ("grp", "loop"), None),
        check_vma=False,
    )
```

profile of v0, /device:TPU:1, one launch (start us, length us, event | category | flops | bytes accessed | tf_op | source)
XLA Modules:
  0.0 231.9 jit_solution(12410850239741031274)
XLA Ops:
  6.5 1.3 convert_reduce_fusion.1
  7.9 1.1 slice_convert_fusion.1
  9.0 1.4 fusion.21
  10.4 0.9 mul.57
  11.3 0.9 add.47
  12.3 0.4 reshape.127
  12.6 0.4 reshape.129
  13.0 0.6 fusion.17
  13.7 16.6 %all_to_all.58 = bf16[8,16,928]{2,0,1:T(8,128)(2,1)S(1)} all-to-all(bf16[8,16,928]{2,0,1:T(8,128)(2,1)S(1)} %get-tuple-element.14), channel_id=1, replica_groups=mesh['grp'=2,'loop'=16] {'loop'}, dimensions={1} | all-to-all | bytes 475136 | tf_op jit(solution)/shard_map/all_to_all | solution.py:41
  30.3 3.8 %fusion.38 = f32[128,1984]{1,0:T(8,128)} fusion(bf16[928,1984]{1,0:T(8,128)(2,1)} %param.14, bf16[8,16,928]{2,0,1:T(8,128)(2,1)S(1)} %all_to_all.58), kind=kOutput, calls=%fused_computation.57 | convolution fusion | flops 471334912 | bytes 4935680 | tf_op jit(solution)/shard_map/dot_general | solution.py:46
  34.1 0.0 reduce-scatter.5.cloned.1.call-update
  34.2 0.0 reduce-scatter.3.cloned.1.call-start
  34.2 13.0 %all_to_all.59 = bf16[8,16,928]{2,0,1:T(8,128)(2,1)S(1)} all-to-all(bf16[8,16,928]{2,0,1:T(8,128)(2,1)S(1)} %get-tuple-element.13), channel_id=1, replica_groups=mesh['grp'=2,'loop'=16] {'loop'}, dimensions={1} | all-to-all | bytes 475136 | tf_op jit(solution)/shard_map/all_to_all | solution.py:41
  47.2 3.9 %fusion.40 = f32[128,1984]{1,0:T(8,128)} fusion(bf16[928,1984]{1,0:T(8,128)(2,1)} %param.14, bf16[8,16,928]{2,0,1:T(8,128)(2,1)S(1)} %all_to_all.59), kind=kOutput, calls=%fused_computation.59 | convolution fusion | flops 471334912 | bytes 4935680 | tf_op jit(solution)/shard_map/dot_general | solution.py:46
  51.1 0.1 iota_compare_fusion
  51.2 36.9 %reduce-scatter.5.cloned.1.call-done = f32[8,1984]{1,0:T(8,128)} async-done(((f32[128,1984]{1,0:T(8,128)}), f32[8,1984]{1,0:T(8,128)}) %reduce-scatter.5.cloned.1.call-update) | async-done | bytes 63504 | tf_op jit(solution)/shard_map/reduce_scatter | solution.py:49
  88.1 0.8 convert_element_type.125
  88.9 0.1 slice_bitcast_fusion.1
  89.0 59.6 %reduce-scatter.3.cloned.1.call-done = f32[8,1984]{1,0:T(8,128)} async-done(((f32[128,1984]{1,0:T(8,128)}), f32[8,1984]{1,0:T(8,128)}) %reduce-scatter.3.cloned.1.call-update) | async-done | bytes 63504 | tf_op jit(solution)/shard_map/reduce_scatter | solution.py:49
  148.6 0.8 convert_element_type.111
  149.4 0.1 slice_bitcast_fusion.3
  149.5 0.1 reshape.126
  149.6 0.2 copy.34
  149.8 0.2 copy.36
  150.0 0.1 reshape.125
  150.1 0.2 copy.28
  150.3 0.2 copy.29
  150.4 0.4 fusion.90
  150.8 0.5 convolution_convert_fusion.3
  151.4 0.1 convert_element_type.114
  151.5 0.4 fusion.93
  152.0 0.6 convolution_convert_fusion.2
  152.6 0.1 convert_element_type.128
  152.7 23.1 %all_gather.7 = bf16[128,1856]{1,0:T(8,128)(2,1)S(1)} all-gather(bf16[8,1856]{1,0:T(8,128)(2,1)S(1)} %convert_element_type.128), channel_id=1, replica_groups=mesh['grp'=2,'loop'=16] {'loop'}, dimensions={0}, use_global_device_ids=true | all-gather | bytes 504832 | tf_op jit(solution)/shard_map/all_gather | solution.py:69
  175.9 3.1 %convolution_convert_fusion = bf16[128,928]{0,1:T(8,128)(2,1)S(1)} fusion(bf16[128,1856]{1,0:T(8,128)(2,1)S(1)} %all_gather.7, bf16[1856,928]{0,1:T(8,128)(2,1)} %param.15), kind=kOutput, calls=%fused_computation.12 | convolution fusion | flops 441044992 | bytes 4157440 | tf_op jit(solution)/shard_map/dot_general | solution.py:70
  179.0 0.8 copy.37
  179.8 3.5 %all-to-all-start.3 = ((bf16[16,8,928]{2,1,0:T(8,128)(2,1)}), bf16[16,8,928]{2,1,0:T(8,128)(2,1)S(1)}, u32[]{:S(2)}, u32[]{:S(2)}) async-start(bf16[16,8,928]{2,1,0:T(8,128)(2,1)} %bitcast.12), calls=%async_computation.5 | async-start | bytes 524288 | tf_op jit(solution)/shard_map/all_to_all | solution.py:73
  183.3 23.3 %all_gather.6 = bf16[128,1856]{1,0:T(8,128)(2,1)S(1)} all-gather(bf16[8,1856]{1,0:T(8,128)(2,1)S(1)} %convert_element_type.114), channel_id=1, replica_groups=mesh['grp'=2,'loop'=16] {'loop'}, dimensions={0}, use_global_device_ids=true | all-gather | bytes 504832 | tf_op jit(solution)/shard_map/all_gather | solution.py:69
  206.6 3.1 %convolution_convert_fusion.1 = bf16[128,928]{0,1:T(8,128)(2,1)S(1)} fusion(bf16[128,1856]{1,0:T(8,128)(2,1)S(1)} %all_gather.6, bf16[1856,928]{0,1:T(8,128)(2,1)} %param.15), kind=kOutput, calls=%fused_computation.13 | convolution fusion | flops 441044992 | bytes 4157440 | tf_op jit(solution)/shard_map/dot_general | solution.py:70
  209.7 0.8 copy.30
  210.6 3.5 %all-to-all-start.1 = ((bf16[16,8,928]{2,1,0:T(8,128)(2,1)}), bf16[16,8,928]{2,1,0:T(8,128)(2,1)S(1)}, u32[]{:S(2)}, u32[]{:S(2)}) async-start(bf16[16,8,928]{2,1,0:T(8,128)(2,1)} %bitcast.5), calls=%async_computation.2 | async-start | bytes 524288 | tf_op jit(solution)/shard_map/all_to_all | solution.py:73
  214.1 0.3 copy.38
  214.4 0.3 reshape.130
  214.7 8.9 %all-to-all-done.1 = bf16[16,8,928]{2,1,0:T(8,128)(2,1)S(1)} async-done(((bf16[16,8,928]{2,1,0:T(8,128)(2,1)}), bf16[16,8,928]{2,1,0:T(8,128)(2,1)S(1)}, u32[]{:S(2)}, u32[]{:S(2)}) %all-to-all-start.1) | async-done | bytes 237600 | tf_op jit(solution)/shard_map/all_to_all | solution.py:73
  223.6 0.3 copy.31
  223.9 0.3 reshape.128
  224.2 0.1 add_convert_fusion.1
  224.3 0.8 copy-done.2
  (22 shorter events, 0.2 us)
Async XLA Ops:
  6.5 81.5 %reduce-scatter.5.cloned.1.call-start = ((), (), s32[]{:S(2)}) async-start(), calls=%async_computation.7 | async-start | bytes 1114112 | tf_op jit(solution)/shard_map/reduce_scatter | solution.py:49
  34.1 17.0 %copy-start.1 = (s32[8]{0:T(128)S(1)}, s32[8]{0:T(128)}, u32[]{:S(2)}) copy-start(s32[8]{0:T(128)} %param.9) | copy-start | bytes 100
  34.2 114.4 %reduce-scatter.3.cloned.1.call-start = ((), (), s32[]{:S(2)}) async-start(), calls=%async_computation.6 | async-start | bytes 1114112 | tf_op jit(solution)/shard_map/reduce_scatter | solution.py:49
  34.2 116.2 %copy-start.4 = (bf16[8,256,64]{1,2,0:T(8,128)(2,1)S(1)}, bf16[8,256,64]{1,2,0:T(8,128)(2,1)}, u32[]{:S(2)}) copy-start(bf16[8,256,64]{1,2,0:T(8,128)(2,1)} %param.10) | copy-start | bytes 786436
  47.2 103.7 %copy-start.3 = (bf16[8,256,64]{1,2,0:T(8,128)(2,1)S(1)}, bf16[8,256,64]{1,2,0:T(8,128)(2,1)}, u32[]{:S(2)}) copy-start(bf16[8,256,64]{1,2,0:T(8,128)(2,1)} %param.11) | copy-start | bytes 786436
  179.8 30.7 %all-to-all-start.3 = ((bf16[16,8,928]{2,1,0:T(8,128)(2,1)}), bf16[16,8,928]{2,1,0:T(8,128)(2,1)S(1)}, u32[]{:S(2)}, u32[]{:S(2)}) async-start(bf16[16,8,928]{2,1,0:T(8,128)(2,1)} %bitcast.12), calls=%async_computation.5 | async-start | bytes 524288 | tf_op jit(solution)/shard_map/all_to_all | solution.py:73
  209.7 14.5 %copy-start = (bf16[2,8,14848]{2,1,0:T(8,128)(2,1)S(1)}, bf16[2,8,14848]{2,1,0:T(8,128)(2,1)}, u32[]{:S(2)}) copy-start(bf16[2,8,14848]{2,1,0:T(8,128)(2,1)} %param.8) | copy-start | bytes 1425412
  210.6 13.0 %all-to-all-start.1 = ((bf16[16,8,928]{2,1,0:T(8,128)(2,1)}), bf16[16,8,928]{2,1,0:T(8,128)(2,1)S(1)}, u32[]{:S(2)}, u32[]{:S(2)}) async-start(bf16[16,8,928]{2,1,0:T(8,128)(2,1)} %bitcast.5), calls=%async_computation.2 | async-start | bytes 524288 | tf_op jit(solution)/shard_map/all_to_all | solution.py:73
  224.3 0.8 copy-start.2
Sparse Core Ops, SparseCore 0:
  34.3 53.7 reduce-scatter.4
  92.1 56.3 reduce-scatter.2
where the time goes:
time: 233 us; the launch traced here: 232 us
  waiting for transfers between devices  105 us (45%)
  blocking collectives  76 us (33%)
  matrix products  15.9 us (7%)
  between operations  13.6 us (6%)
  local copies, waits for them, and re-layouts  7.6 us (3%)
  starting transfers between devices  7.01 us (3%)
  other arithmetic  6.42 us (3%)
    reduce_scatter x2, waiting for transfers between devices, local(): lax.psum_scatter(one_term(jnp.int32(0), local_rows * lax.axis_size('loop'...  96.5 us
    all_gather x2, blocking collectives, local(): every_row = lax.all_gather(mixed_heads, 'loop', axis=0, tiled=True)  46.4 us
    all_to_all x2, blocking collectives, local(): lax.all_to_all(normed_list[step_index], 'loop', split_axis=1, concat_axis...  29.6 us
    all_to_all x2, waiting for transfers between devices, local(): lax.all_to_all(columns_out, 'loop', split_axis=0, concat_axis=1, tiled=True)  8.91 us
    dot_general x2, matrix products, one_term(): return jnp.dot(source, w_qkv, preferred_element_type=jnp.float32)  7.72 us
    all_to_all x2, starting transfers between devices, local(): lax.all_to_all(columns_out, 'loop', split_axis=0, concat_axis=1, tiled=True)  6.97 us
    dot_general x2, matrix products, local(): jnp.dot(every_row, w_out, preferred_element_type=jnp.float32)  6.2 us
  transfers between devices with their start and end apart: 4, of which 3 were waited for; matrix products, arithmetic and copies ran while one was open for 4% of the time, Pallas kernels for 0%

commit v1 on v0

v1 whole, which is shorter than its diff:
```python
import jax
import jax.numpy as jnp
from jax import lax
from jax.sharding import PartitionSpec as P


def layer_norm(current, ln_gain, ln_bias):
    values = current.astype(jnp.float32)
    average = jnp.mean(values, axis=-1, keepdims=True)
    centred = values - average
    variance = jnp.mean(centred * centred, axis=-1, keepdims=True)
    return (centred * lax.rsqrt(variance + 1e-05) * ln_gain + ln_bias).astype(jnp.bfloat16)


def attend(queries, fresh_keys, fresh_values, cache_keys, cache_values, lengths):
    rows, steps, heads, head_dim = queries.shape
    context = cache_keys.shape[1]
    flat = queries.reshape(rows, steps * heads, head_dim)
    seen = jnp.arange(context, dtype=jnp.int32)[None, :] < lengths[:, None]
    old = jnp.einsum("rqe,rpe->rqp", flat, cache_keys, preferred_element_type=jnp.float32) * 0.125
    old = jnp.where(seen[:, None, :], old, -1e30)
    new = jnp.einsum("rqe,rte->rqt", flat, fresh_keys, preferred_element_type=jnp.float32) * 0.125
    step_of = jnp.arange(steps * heads, dtype=jnp.int32)[:, None] // heads
    seen_new = jnp.arange(steps, dtype=jnp.int32)[None, :] <= step_of
    new = jnp.where(seen_new[None], new, -1e30)
    maxima = jnp.maximum(
        jnp.max(old, axis=-1, keepdims=True), jnp.max(new, axis=-1, keepdims=True)
    )
    exp_old = jnp.exp(old - maxima)
    exp_new = jnp.exp(new - maxima)
    totals = jnp.sum(exp_old, axis=-1, keepdims=True) + jnp.sum(exp_new, axis=-1, keepdims=True)
    prob_old = (exp_old / totals).astype(jnp.bfloat16)
    prob_new = (exp_new / totals).astype(jnp.bfloat16)
    mixed = jnp.einsum("rqp,rpe->rqe", prob_old, cache_values, preferred_element_type=jnp.float32)
    mixed += jnp.einsum("rqt,rte->rqe", prob_new, fresh_values, preferred_element_type=jnp.float32)
    return mixed.reshape(rows, steps, heads * head_dim).astype(jnp.bfloat16)


def local(hidden, lengths, cache_keys, cache_values, ln_gain, ln_bias, w_qkv, w_out):
    steps, rows, width = hidden.shape
    head_dim = cache_keys.shape[2]
    heads = w_qkv.shape[1] // head_dim - 2
    count = lax.axis_size("loop")
    part = width // count
    normed = layer_norm(hidden, ln_gain, ln_bias).reshape(steps * rows, width)
    spread = lax.all_to_all(normed, "loop", split_axis=1, concat_axis=0, tiled=True)
    terms = jnp.dot(spread, w_qkv, preferred_element_type=jnp.float32).astype(jnp.bfloat16)
    terms = terms.reshape(count, steps * rows, -1)
    arrived = lax.all_to_all(terms, "loop", split_axis=0, concat_axis=0, tiled=True)
    projected = jnp.sum(arrived.astype(jnp.float32), axis=0).astype(jnp.bfloat16)
    projected = projected.reshape(steps, rows, -1).transpose(1, 0, 2)
    queries = projected[:, :, : heads * head_dim].reshape(rows, steps, heads, head_dim)
    fresh_keys = projected[:, :, heads * head_dim : (heads + 1) * head_dim]
    fresh_values = projected[:, :, (heads + 1) * head_dim :]
    mixed = attend(queries, fresh_keys, fresh_values, cache_keys, cache_values, lengths)
    mixed = mixed.transpose(1, 0, 2).reshape(steps * rows, -1)
    every_row = lax.all_gather(mixed, "loop", axis=0, tiled=True)
    columns = jnp.dot(every_row, w_out, preferred_element_type=jnp.float32).astype(jnp.bfloat16)
    attention = lax.all_to_all(columns, "loop", split_axis=0, concat_axis=1, tiled=True)
    attention = attention.reshape(steps, rows, width)
    return (hidden.astype(jnp.float32) + attention.astype(jnp.float32)).astype(jnp.bfloat16)


def solution(mesh):
    return jax.shard_map(
        local,
        mesh=mesh,
        in_specs=(
            P(None, ("grp", "loop"), None),
            P(("grp", "loop")),
            P(("grp", "loop"), None, None),
            P(("grp", "loop"), None, None),
            P(),
            P(),
            P("loop", None),
            P(None, "loop"),
        ),
        out_specs=P(None, ("grp", "loop"), None),
        check_vma=False,
    )
```

time: 233 us -> 110 us (0.47)
  waiting for transfers between devices: 105 us -> 23 us
  between operations: 13.6 us -> 0.21 us
  blocking collectives: 76 us -> 63.3 us
  matrix products: 15.9 us -> 8.08 us
  local copies, waits for them, and re-layouts: 7.6 us -> 4.3 us
  starting transfers between devices: 7.01 us -> 4.5 us
    reduce_scatter x2 -> x0, waiting for transfers between devices: 96.5 us -> none  [local(): lax.psum_scatter(one_term(jnp.int32(0), local_rows * lax.axis_size('loop'...]
    all_gather x2 -> x1, blocking collectives: 46.4 us -> 25.2 us  [local(): every_row = lax.all_gather(mixed, 'loop', axis=0, tiled=True)]
    all_to_all x2 -> x1, waiting for transfers between devices: 8.91 us -> 23 us  [local(): lax.all_to_all(terms, 'loop', split_axis=0, concat_axis=0, tiled=True)]
    all_to_all x2, blocking collectives: 29.6 us -> 38.1 us  [the longest x1 21.2 us: local(): lax.all_to_all(normed, 'loop', split_axis=1, concat_axis=0, tiled=True)]
    dot_general x4 -> x5, matrix products: 8.9 us -> 4.88 us  [the longest x1 3.79 us: local(): jnp.dot(spread, w_qkv, preferred_element_type=jnp.float32)]
    dot_general x2 -> x1, matrix products: 6.2 us -> 3.19 us  [local(): jnp.dot(every_row, w_out, preferred_element_type=jnp.float32)]
    all_to_all x2 -> x1, starting transfers between devices: 6.97 us -> 4.5 us  [local(): lax.all_to_all(terms, 'loop', split_axis=0, concat_axis=0, tiled=True)]
  transfers between devices with their start and end apart: 4 -> 1, of which waited for: 3 -> 1; matrix products, arithmetic and copies ran while one was open for 4% -> 0% of each run, Pallas kernels for 0% -> 0%
where the time goes in v1:
time: 110 us; the launch traced here: 109 us
  blocking collectives  63.3 us (58%)
  waiting for transfers between devices  23 us (21%)
  matrix products  8.08 us (7%)
  other arithmetic  5.43 us (5%)
  starting transfers between devices  4.5 us (4%)
  local copies, waits for them, and re-layouts  4.3 us (4%)
    all_gather x1, blocking collectives, local(): every_row = lax.all_gather(mixed, 'loop', axis=0, tiled=True)  25.2 us
    all_to_all x1, waiting for transfers between devices, local(): lax.all_to_all(terms, 'loop', split_axis=0, concat_axis=0, tiled=True)  23 us
    all_to_all x1, blocking collectives, local(): lax.all_to_all(normed, 'loop', split_axis=1, concat_axis=0, tiled=True)  21.2 us
    all_to_all x1, blocking collectives, local(): lax.all_to_all(columns, 'loop', split_axis=0, concat_axis=1, tiled=True)  16.9 us
    all_to_all x1, starting transfers between devices, local(): lax.all_to_all(terms, 'loop', split_axis=0, concat_axis=0, tiled=True)  4.5 us
    dot_general x1, matrix products, local(): jnp.dot(spread, w_qkv, preferred_element_type=jnp.float32)  3.79 us
    dot_general x1, matrix products, local(): jnp.dot(every_row, w_out, preferred_element_type=jnp.float32)  3.19 us
  transfers between devices with their start and end apart: 1, of which 1 were waited for; matrix products, arithmetic and copies ran while one was open for 0% of the time, Pallas kernels for 0%

profile of v1, /device:TPU:1, one launch (start us, length us, event | category | flops | bytes accessed | tf_op | source)
XLA Modules:
  0.0 108.9 jit_solution(5189469483731483823)
XLA Ops:
  0.0 0.0 copy-start
  0.0 1.3 %convert_reduce_fusion = f32[2,8]{1,0:T(2,128)S(1)} fusion(bf16[2,8,14848]{2,1,0:T(8,128)(2,1)} %param.8), kind=kLoop, calls=%fused_computation.3 | loop fusion | flops 475120 | bytes 475200 | tf_op jit(solution)/shard_map/reduce_sum | solution.py:9
  1.3 1.3 %fusion.5 = f32[2,8]{1,0:T(2,128)S(1)} fusion(bf16[2,8,14848]{2,1,0:T(8,128)(2,1)} %param.8, f32[2,8]{1,0:T(2,128)S(1)} %broadcast_multiply_fusion), kind=kLoop, calls=%fused_computation.14 | loop fusion | flops 950256 | bytes 475264 | tf_op jit(solution)/shard_map/reduce_sum | solution.py:11
  2.6 1.3 %fusion.8 = bf16[2,8,14848]{2,1,0:T(8,128)(2,1)S(1)} fusion(bf16[2,8,14848]{2,1,0:T(8,128)(2,1)} %param.8, f32[14848]{0:T(1024)} %param.13, f32[14848]{0:T(1024)} %param.12, f32[2,8]{1,0:T(2,128)S(1)} %add_rsqrt_fusion, f32[2,8]{1,0:T(2,128)S(1)} %broadcast_multiply_fusion), kind=kLoop, calls=%fused_computation.17 | loop fusion | flops 1425408 | bytes 1069184 | tf_op jit(solution)/shard_map/convert_element_type | solution.py:12
  3.9 0.8 all_to_all.27
  4.8 0.3 copy.15
  5.1 21.2 %all_to_all.37 = bf16[16,16,928]{2,0,1:T(8,128)(2,1)S(1)} all-to-all(bf16[16,16,928]{2,0,1:T(8,128)(2,1)S(1)} %copy.15), channel_id=1, replica_groups=mesh['grp'=2,'loop'=16] {'loop'}, dimensions={1} | all-to-all | bytes 950272 | tf_op jit(solution)/shard_map/all_to_all | solution.py:46
  26.3 3.8 %convolution_convert_fusion = bf16[256,1984]{0,1:T(8,128)(2,1)S(1)} fusion(bf16[256,928]{1,0:T(8,128)(2,1)S(1)} %bitcast.24, bf16[928,1984]{1,0:T(8,128)(2,1)} %param.14), kind=kOutput, calls=%fused_computation | convolution fusion | flops 943177728 | bytes 5173248 | tf_op jit(solution)/shard_map/dot_general | solution.py:47
  30.1 0.0 copy-start.2
  30.1 0.0 copy-start.3
  30.1 1.4 %copy.16 = bf16[256,1984]{1,0:T(8,128)(2,1)} copy(bf16[256,1984]{0,1:T(8,128)(2,1)S(1)} %convolution_convert_fusion) | data formatting | bytes 2031616 | tf_op jit(solution)/shard_map/convert_element_type | solution.py:47
  31.5 4.5 %all-to-all-start.1 = ((bf16[16,16,1984]{2,1,0:T(8,128)(2,1)}), bf16[16,16,1984]{2,1,0:T(8,128)(2,1)S(1)}, u32[]{:S(2)}, u32[]{:S(2)}) async-start(bf16[16,16,1984]{2,1,0:T(8,128)(2,1)} %bitcast.2), calls=%async_computation.1 | async-start | bytes 2097152 | tf_op jit(solution)/shard_map/all_to_all | solution.py:49
  36.1 0.0 copy-done.2
  36.1 0.1 iota_compare_fusion
  36.1 23.0 %all-to-all-done.1 = bf16[16,16,1984]{2,1,0:T(8,128)(2,1)S(1)} async-done(((bf16[16,16,1984]{2,1,0:T(8,128)(2,1)}), bf16[16,16,1984]{2,1,0:T(8,128)(2,1)S(1)}, u32[]{:S(2)}, u32[]{:S(2)}) %all-to-all-start.1) | async-done | bytes 1015840 | tf_op jit(solution)/shard_map/all_to_all | solution.py:49
  59.2 0.2 reduce_sum.50
  59.3 0.1 copy.23
  59.5 0.1 reshape_reshape.3
  59.6 0.2 fusion.20
  59.9 0.0 copy-done
  59.9 0.3 fusion.19
  60.2 0.3 fusion.10
  60.5 0.2 fusion.14
  60.7 0.0 copy-done.3
  60.7 0.3 fusion.1
  61.1 0.1 convert_element_type.45
  61.2 25.2 %all_gather.3 = bf16[256,1856]{1,0:T(8,128)(2,1)S(1)} all-gather(bf16[16,1856]{1,0:T(8,128)(2,1)S(1)} %bitcast.30), channel_id=1, replica_groups=mesh['grp'=2,'loop'=16] {'loop'}, dimensions={0}, use_global_device_ids=true | all-gather | bytes 1009664 | tf_op jit(solution)/shard_map/all_gather | solution.py:57
  86.5 3.2 %convolution_convert_fusion.1 = bf16[256,928]{0,1:T(8,128)(2,1)S(1)} fusion(bf16[256,1856]{1,0:T(8,128)(2,1)S(1)} %all_gather.3, bf16[1856,928]{0,1:T(8,128)(2,1)} %param.15), kind=kOutput, calls=%fused_computation.4 | convolution fusion | flops 882089984 | bytes 4870144 | tf_op jit(solution)/shard_map/dot_general | solution.py:58
  89.7 0.2 copy.19
  89.9 0.0 copy-start.1
  89.9 16.9 %all_to_all.38 = bf16[16,16,928]{2,1,0:T(8,128)(2,1)S(1)} all-to-all(bf16[16,16,928]{2,1,0:T(8,128)(2,1)S(1)} %bitcast.23), channel_id=1, replica_groups=mesh['grp'=2,'loop'=16] {'loop'}, dimensions={0} | all-to-all | bytes 950272 | tf_op jit(solution)/shard_map/all_to_all | solution.py:59
  106.8 0.1 convert_bitcast_fusion
  106.9 0.6 copy.20
  107.5 0.5 reshape.111
  108.0 0.0 copy-done.1
  108.0 0.9 fusion.9
  (9 shorter events, 0.1 us)
Async XLA Ops:
  0.0 59.9 %copy-start = (bf16[8,256,64]{1,2,0:T(8,128)(2,1)S(1)}, bf16[8,256,64]{1,2,0:T(8,128)(2,1)}, u32[]{:S(2)}) copy-start(bf16[8,256,64]{1,2,0:T(8,128)(2,1)} %param.10) | copy-start | bytes 786436
  30.1 6.0 %copy-start.2 = (s32[8]{0:T(128)S(1)}, s32[8]{0:T(128)}, u32[]{:S(2)}) copy-start(s32[8]{0:T(128)} %param.9) | copy-start | bytes 100
  30.1 30.7 %copy-start.3 = (bf16[8,256,64]{1,2,0:T(8,128)(2,1)S(1)}, bf16[8,256,64]{1,2,0:T(8,128)(2,1)}, u32[]{:S(2)}) copy-start(bf16[8,256,64]{1,2,0:T(8,128)(2,1)} %param.11) | copy-start | bytes 786436
  31.5 27.6 %all-to-all-start.1 = ((bf16[16,16,1984]{2,1,0:T(8,128)(2,1)}), bf16[16,16,1984]{2,1,0:T(8,128)(2,1)S(1)}, u32[]{:S(2)}, u32[]{:S(2)}) async-start(bf16[16,16,1984]{2,1,0:T(8,128)(2,1)} %bitcast.2), calls=%async_computation.1 | async-start | bytes 2097152 | tf_op jit(solution)/shard_map/all_to_all | solution.py:49
  89.9 18.1 %copy-start.1 = (bf16[2,8,14848]{2,1,0:T(8,128)(2,1)S(1)}, bf16[2,8,14848]{2,1,0:T(8,128)(2,1)}, u32[]{:S(2)}) copy-start(bf16[2,8,14848]{2,1,0:T(8,128)(2,1)} %param.8) | copy-start | bytes 1425412

commit v2 on v1

--- a/solution.py
+++ b/solution.py
@@ -1,15 +1,311 @@
+import functools
+
 import jax
 import jax.numpy as jnp
 from jax import lax
+from jax.experimental import pallas as pl
+from jax.experimental.pallas import tpu as pltpu
 from jax.sharding import PartitionSpec as P
 
-
-def layer_norm(current, ln_gain, ln_bias):
-    values = current.astype(jnp.float32)
-    average = jnp.mean(values, axis=-1, keepdims=True)
+MESH = pl.DeviceIdType.MESH
+VMEM = pltpu.VMEM
+DMA = pltpu.SemaphoreType.DMA
+
+
+def hail(devices):
+    barrier = pltpu.get_barrier_semaphore()
+    for device in devices:
+        pl.semaphore_signal(barrier, inc=1, device_id={"loop": device}, device_id_type=MESH)
+
+
+def meet(devices):
+    pl.semaphore_wait(pltpu.get_barrier_semaphore(), len(devices))
+
+
+def remote(src, dst, send_sem, recv_sem, device):
+    return pltpu.make_async_remote_copy(
+        src_ref=src,
+        dst_ref=dst,
+        send_sem=send_sem,
+        recv_sem=recv_sem,
+        device_id={"loop": device},
+        device_id_type=MESH,
+    )
+
+
+def far_first(count):
+    return sorted(range(1, count), key=lambda k: abs(2 * k - count))
+
+
+def product(left, weights, store):
+    width = weights.shape[1]
+    for low in range(0, width, 512):
+        high = min(low + 512, width)
+        store(
+            low,
+            high,
+            jnp.dot(left, weights[:, low:high], preferred_element_type=jnp.float32),
+        )
+
+
+def project_kernel(
+    count,
+    h_ref,
+    gain_ref,
+    bias_ref,
+    w_hbm,
+    o_ref,
+    w_ref,
+    normed,
+    spread,
+    terms,
+    sib,
+    packed,
+    arrived,
+    w_sem,
+    send_x,
+    recv_x,
+    send_a,
+    recv_a,
+    send_b,
+    recv_b,
+):
+    me = lax.axis_index("loop")
+    chips = count // 2
+    core = lax.rem(me, 2)
+    chip = me // 2
+    other = 1 - core
+    sibling = chip * 2 + other
+    part = w_ref.shape[0]
+    rows, width = h_ref.shape
+    far = far_first(count)
+    everyone = [lax.rem(me + k, count) for k in far]
+    hail(everyone)
+    w_copy = pltpu.make_async_copy(w_hbm, w_ref, w_sem)
+    w_copy.start()
+    values = h_ref[...].astype(jnp.float32)
+    average = jnp.sum(values, axis=-1, keepdims=True) / width
     centred = values - average
-    variance = jnp.mean(centred * centred, axis=-1, keepdims=True)
-    return (centred * lax.rsqrt(variance + 1e-05) * ln_gain + ln_bias).astype(jnp.bfloat16)
+    variance = jnp.sum(centred * centred, axis=-1, keepdims=True) / width
+    scale = lax.rsqrt(variance + 1e-05)
+    for d in range(count):
+        at = slice(d * part, (d + 1) * part)
+        block = (h_ref[:, at].astype(jnp.float32) - average) * scale
+        normed[d] = (block * gain_ref[:, at] + bias_ref[:, at]).astype(jnp.bfloat16)
+    meet(everyone)
+    copies = []
+    for k in far:
+        to = lax.rem(me + k, count)
+        copy = remote(normed.at[to], spread.at[core, chip], send_x.at[k], recv_x.at[k], to)
+        copy.start()
+        copies.append(copy)
+    spread[core, chip] = normed[me]
+    w_copy.wait()
+    for k in far:
+        sender = lax.rem(me + count - k, count)
+        block = spread.at[lax.rem(sender, 2), sender // 2]
+        remote(block, block, send_x.at[k], recv_x.at[k], sender).wait_recv()
+
+    def multiply(which):
+        def store(low, high, tile):
+            terms[which, :, :, low:high] = tile.reshape(chips, rows, high - low)
+
+        product(spread[which].reshape(chips * rows, part), w_ref, store)
+
+    multiply(other)
+    order = far_first(chips)
+    firsts = {}
+    for k in order + [0]:
+        j = lax.rem(chip + k, chips)
+        firsts[k] = remote(terms.at[other, j], sib.at[j], send_a.at[k], recv_a.at[k], sibling)
+        firsts[k].start()
+    multiply(core)
+    for k in order:
+        j = lax.rem(chip + k, chips)
+        firsts[k].wait_recv()
+        packed[j] = (terms[core, j] + sib[j]).astype(jnp.bfloat16)
+        copy = remote(packed.at[j], arrived.at[chip], send_b.at[k], recv_b.at[k], j * 2 + core)
+        copy.start()
+        copies.append(copy)
+    firsts[0].wait_recv()
+    total = terms[core, chip] + sib[chip]
+    for k in order[::-1]:
+        sender = lax.rem(chip + chips - k, chips)
+        block = arrived.at[sender]
+        remote(block, block, send_b.at[k], recv_b.at[k], sender * 2 + core).wait_recv()
+        total = total + arrived[sender].astype(jnp.float32)
+    o_ref[...] = total.astype(jnp.bfloat16)
+    for copy in list(firsts.values()) + copies:
+        copy.wait_send()
+
+
+def call(kernel, out, specs, scratch, collective_id, *args):
+    return pl.pallas_call(
+        kernel,
+        out_shape=out,
+        in_specs=[pl.BlockSpec(memory_space=space) for space in specs],
+        out_specs=pl.BlockSpec(memory_space=VMEM),
+        scratch_shapes=scratch,
+        compiler_params=pltpu.CompilerParams(
+            collective_id=collective_id, has_side_effects=True, vmem_limit_bytes=48 * 2**20
+        ),
+    )(*args)
+
+
+def project(hidden, ln_gain, ln_bias, w_qkv, count, collective_id):
+    rows = hidden.shape[0]
+    part, width = w_qkv.shape
+    chips = count // 2
+    half = jnp.bfloat16
+    return call(
+        functools.partial(project_kernel, count),
+        jax.ShapeDtypeStruct((rows, width), half),
+        [VMEM, VMEM, VMEM, pl.ANY],
+        [
+            VMEM((part, width), half),
+            VMEM((count, rows, part), half),
+            VMEM((2, chips, rows, part), half),
+            VMEM((2, chips, rows, width), jnp.float32),
+            VMEM((chips, rows, width), jnp.float32),
+            VMEM((chips, rows, width), half),
+            VMEM((chips, rows, width), half),
+            DMA,
+        ]
+        + [DMA((count,))] * 2
+        + [DMA((chips,))] * 4,
+        collective_id,
+        hidden,
+        ln_gain,
+        ln_bias,
+        w_qkv,
+    )
+
+
+def output_kernel(
+    count,
+    m_ref,
+    w_hbm,
+    o_ref,
+    w_ref,
+    heads,
+    columns,
+    w_sem,
+    send_a,
+    recv_a,
+    send_y,
+    recv_y,
+    send_s,
+    recv_s,
+    send_x,
+    recv_x,
+):
+    me = lax.axis_index("loop")
+    core = lax.rem(me, 2)
+    chip = me // 2
+    other = 1 - core
+    chips = count // 2
+    pairs = chips // 2
+    pair = chip // 2
+    side = lax.rem(chip, 2)
+    sibling = chip * 2 + other
+    partner = (pair * 2 + 1 - side) * 2 + core
+    rows, depth = m_ref.shape
+    everyone = [lax.rem(me + k, count) for k in far_first(count)]
+    hail(everyone)
+    w_copy = pltpu.make_async_copy(w_hbm, w_ref, w_sem)
+    w_copy.start()
+    meet(everyone)
+    order = far_first(pairs)[::-1]
+    mine = heads.at[core, chip]
+    copies = []
+
+    def push(copy):
+        copy.start()
+        copies.append(copy)
+
+    push(remote(m_ref, mine, send_y.at[0], recv_y.at[0], partner))
+    for k in order[::-1]:
+        to = (lax.rem(pair + k, pairs) * 2 + side) * 2 + core
+        push(remote(m_ref, mine, send_a.at[k], recv_a.at[k], to))
+    push(remote(m_ref, mine, send_s.at[0], recv_s.at[0], sibling))
+    heads[core, chip] = m_ref[...]
+    source = pair * 2 + 1 - side
+    block = heads.at[core, source]
+    remote(block, block, send_y.at[0], recv_y.at[0], partner).wait_recv()
+    push(remote(block, block, send_s.at[pairs], recv_s.at[pairs], sibling))
+    for k in order:
+        source = lax.rem(pair + pairs - k, pairs) * 2 + side
+        block = heads.at[core, source]
+        remote(block, block, send_a.at[k], recv_a.at[k], partner).wait_recv()
+        push(remote(block, block, send_y.at[k], recv_y.at[k], partner))
+        push(remote(block, block, send_s.at[k], recv_s.at[k], sibling))
+    for k in order:
+        source = lax.rem(pair + pairs - k, pairs) * 2 + 1 - side
+        block = heads.at[core, source]
+        remote(block, block, send_y.at[k], recv_y.at[k], partner).wait_recv()
+        push(remote(block, block, send_s.at[pairs + k], recv_s.at[pairs + k], sibling))
+    w_copy.wait()
+
+    def multiply(which):
+        def store(low, high, tile):
+            columns[which, :, :, low:high] = tile.astype(jnp.bfloat16).reshape(
+                chips, rows, high - low
+            )
+
+        product(heads[which].reshape(chips * rows, depth), w_ref, store)
+
+    spans = far_first(chips)
+    multiply(core)
+    for k in spans:
+        j = lax.rem(chip + k, chips)
+        sems = send_x.at[k], recv_x.at[k]
+        push(remote(columns.at[core, j], o_ref.at[me], *sems, j * 2 + core))
+    o_ref[me] = columns[core, chip]
+    for far in range(2):
+        for k in [0] + order:
+            source = lax.rem(pair + pairs - k, pairs) * 2 + (1 - side if far else side)
+            block = heads.at[other, source]
+            sem = far * pairs + k
+            remote(block, block, send_s.at[sem], recv_s.at[sem], sibling).wait_recv()
+    multiply(other)
+    for k in spans + [0]:
+        j = lax.rem(chip + k, chips)
+        sems = send_x.at[chips + k], recv_x.at[chips + k]
+        push(remote(columns.at[other, j], o_ref.at[me], *sems, j * 2 + other))
+    for k in spans:
+        sender = lax.rem(chip + chips - k, chips) * 2 + core
+        block = o_ref.at[sender]
+        remote(block, block, send_x.at[k], recv_x.at[k], sender).wait_recv()
+    for k in spans + [0]:
+        sender = lax.rem(chip + chips - k, chips) * 2 + other
+        block = o_ref.at[sender]
+        remote(block, block, send_x.at[chips + k], recv_x.at[chips + k], sender).wait_recv()
+    for copy in copies:
+        copy.wait_send()
+
+
+def output(mixed, w_out, count, collective_id):
+    rows, depth = mixed.shape
+    part = w_out.shape[1]
+    chips = count // 2
+    half = jnp.bfloat16
+    return call(
+        functools.partial(output_kernel, count),
+        jax.ShapeDtypeStruct((count, rows, part), half),
+        [VMEM, pl.ANY],
+        [
+            VMEM((depth, part), half),
+            VMEM((2, chips, rows, depth), half),
+            VMEM((2, chips, rows, part), half),
+            DMA,
+        ]
+        + [DMA((chips // 2,))] * 4
+        + [DMA((chips,))] * 2
+        + [DMA((count,))] * 2,
+        collective_id,
+        mixed,
+        w_out,
+    )
 
 
 def attend(queries, fresh_keys, fresh_values, cache_keys, cache_values, lengths):
@@ -41,23 +337,18 @@
     head_dim = cache_keys.shape[2]
     heads = w_qkv.shape[1] // head_dim - 2
     count = lax.axis_size("loop")
-    part = width // count
-    normed = layer_norm(hidden, ln_gain, ln_bias).reshape(steps * rows, width)
-    spread = lax.all_to_all(normed, "loop", split_axis=1, concat_axis=0, tiled=True)
-    terms = jnp.dot(spread, w_qkv, preferred_element_type=jnp.float32).astype(jnp.bfloat16)
-    terms = terms.reshape(count, steps * rows, -1)
-    arrived = lax.all_to_all(terms, "loop", split_axis=0, concat_axis=0, tiled=True)
-    projected = jnp.sum(arrived.astype(jnp.float32), axis=0).astype(jnp.bfloat16)
+    both = steps * rows
+    projected = project(
+        hidden.reshape(both, width), ln_gain[None], ln_bias[None], w_qkv, count, 0
+    )
     projected = projected.reshape(steps, rows, -1).transpose(1, 0, 2)
     queries = projected[:, :, : heads * head_dim].reshape(rows, steps, heads, head_dim)
     fresh_keys = projected[:, :, heads * head_dim : (heads + 1) * head_dim]
     fresh_values = projected[:, :, (heads + 1) * head_dim :]
     mixed = attend(queries, fresh_keys, fresh_values, cache_keys, cache_values, lengths)
     mixed = mixed.transpose(1, 0, 2).reshape(steps * rows, -1)
-    every_row = lax.all_gather(mixed, "loop", axis=0, tiled=True)
-    columns = jnp.dot(every_row, w_out, preferred_element_type=jnp.float32).astype(jnp.bfloat16)
-    attention = lax.all_to_all(columns, "loop", split_axis=0, concat_axis=1, tiled=True)
-    attention = attention.reshape(steps, rows, width)
+    attention = output(mixed, w_out, count, 1)
+    attention = attention.transpose(1, 0, 2).reshape(steps, rows, width)
     return (hidden.astype(jnp.float32) + attention.astype(jnp.float32)).astype(jnp.bfloat16)
 
 

time: 110 us -> 78.1 us (0.71)
  blocking collectives: 63.3 us -> 0 us
  Pallas kernels: 0 us -> 59.8 us
  waiting for transfers between devices: 23 us -> 0 us
  local copies, waits for them, and re-layouts: 4.3 us -> 14.5 us
  matrix products: 8.08 us -> 1.09 us
  starting transfers between devices: 4.5 us -> 0 us
  other arithmetic: 5.43 us -> 2.06 us
    pallas_call x0 -> x2, Pallas kernels: none -> 59.8 us  [call(): pl.pallas_call(kernel, out_shape=out, in_specs=[pl.BlockSpec(memory_space...]
    all_to_all x2 -> x0, blocking collectives: 38.1 us -> none  [the longest x1 21.2 us: local(): lax.all_to_all(normed, 'loop', split_axis=1, concat_axis=0, tiled=True)]
    all_gather x1 -> x0, blocking collectives: 25.2 us -> none  [local(): every_row = lax.all_gather(mixed, 'loop', axis=0, tiled=True)]
    all_to_all x1 -> x0, waiting for transfers between devices: 23 us -> none  [local(): lax.all_to_all(terms, 'loop', split_axis=0, concat_axis=0, tiled=True)]
    unnamed x8 -> x13, local copies, waits for them, and re-layouts: 0.02 us -> 11.2 us
    dot_general x2 -> x0, matrix products: 6.98 us -> none  [the longest x1 3.79 us: local(): jnp.dot(spread, w_qkv, preferred_element_type=jnp.float32)]
    all_to_all x1 -> x0, starting transfers between devices: 4.5 us -> none  [local(): lax.all_to_all(terms, 'loop', split_axis=0, concat_axis=0, tiled=True)]
    reduce_sum x3 -> x0, other arithmetic: 2.75 us -> none  [the longest x1 1.33 us: layer_norm(): variance = jnp.mean(centred * centred, axis=-1, keepdims=True)]
  transfers between devices with their start and end apart: 1 -> 0, of which waited for: 1 -> 0; matrix products, arithmetic and copies ran while one was open for 0% -> 0% of each run, Pallas kernels for 0% -> 0%
where the time goes in v2:
time: 78.1 us; the launch traced here: 77.6 us
  Pallas kernels  59.8 us (77%)
  local copies, waits for them, and re-layouts  14.5 us (19%)
  other arithmetic  2.06 us (3%)
  matrix products  1.09 us (1%)
    pallas_call x2, Pallas kernels, call(): pl.pallas_call(kernel, out_shape=out, in_specs=[pl.BlockSpec(memory_space...  59.8 us
    unnamed x13, local copies, waits for them, and re-layouts  11.2 us

profile of v2, /device:TPU:1, one launch (start us, length us, event | category | flops | bytes accessed | tf_op | source)
XLA Modules:
  0.0 77.6 jit_solution(17777454221134206298)
XLA Ops:
  0.0 0.0 copy-start
  0.0 0.8 iota_compare_fusion
  0.8 0.9 %broadcast_in_dim.41.gain_ref = f32[1,14848]{1,0:T(1,128)S(1)} reshape(f32[14848]{0:T(1024)} %param.12) | data formatting | bytes 118784 | tf_op jit(solution)/shard_map/broadcast_in_dim | solution.py:342
  1.7 0.9 %broadcast_in_dim.42.bias_ref = f32[1,14848]{1,0:T(1,128)S(1)} reshape(f32[14848]{0:T(1024)} %param.13) | data formatting | bytes 118784 | tf_op jit(solution)/shard_map/broadcast_in_dim | solution.py:342
  2.5 0.0 copy-start.2
  2.6 2.1 %copy-done.2 = bf16[928,1984]{1,0:T(8,128)(2,1)S(1)} copy-done((bf16[928,1984]{1,0:T(8,128)(2,1)S(1)}, bf16[928,1984]{1,0:T(8,128)(2,1)}, u32[]{:S(2)}) %copy-start.2) | copy-done | bytes 3682328
  4.6 0.0 copy-start.3
  4.6 1.0 %copy-done.3 = bf16[2,8,14848]{2,1,0:T(8,128)(2,1)S(1)} copy-done((bf16[2,8,14848]{2,1,0:T(8,128)(2,1)S(1)}, bf16[2,8,14848]{2,1,0:T(8,128)(2,1)}, u32[]{:S(2)}) %copy-start.3) | copy-done | bytes 475160
  5.6 0.0 copy-start.5
  5.6 31.7 %shard_map.82 = bf16[16,1984]{1,0:T(8,128)(2,1)S(1)} custom-call(bf16[16,14848]{1,0:T(8,128)(2,1)S(1)} %bitcast.15, f32[1,14848]{1,0:T(1,128)S(1)} %broadcast_in_dim.41.gain_ref, f32[1,14848]{1,0:T(1,128)S(1)} %broadcast_in_dim.42.bias_ref, bf16[928,1984]{1,0:T(8,128)(2,1)S(1)} %copy-done.2), custom_call_target="tpu_custom_call" | custom-call | tf_op jit(solution)/shard_map/pallas_call | solution.py:143
  37.3 0.1 copy.18
  37.5 0.1 reshape_reshape.3
  37.6 0.2 fusion.13
  37.9 0.0 copy-done
  37.9 0.3 fusion.12
  38.2 0.3 fusion.3
  38.5 0.2 fusion.7
  38.7 0.0 copy-done.5
  38.8 0.3 fusion.1
  39.1 0.1 convert_element_type.31
  39.3 6.1 %copy.14.w_hbm = bf16[1856,928]{1,0:T(8,128)(2,1)} copy(bf16[1856,928]{0,1:T(8,128)(2,1)} %param.15) | data formatting | bytes 6889472 | tf_op args[7]
  45.3 0.0 copy-start.1
  45.3 2.1 %copy-done.1 = bf16[1856,928]{1,0:T(8,128)(2,1)S(1)} copy-done((bf16[1856,928]{1,0:T(8,128)(2,1)S(1)}, bf16[1856,928]{1,0:T(8,128)(2,1)}, u32[]{:S(2)}) %copy-start.1) | copy-done | bytes 3444760
  47.4 28.1 %shard_map.83 = bf16[16,16,928]{2,1,0:T(8,128)(2,1)S(1)} custom-call(bf16[16,1856]{1,0:T(8,128)(2,1)S(1)} %bitcast.17, bf16[1856,928]{1,0:T(8,128)(2,1)S(1)} %copy-done.1), custom_call_target="tpu_custom_call" | custom-call | tf_op jit(solution)/shard_map/pallas_call | solution.py:143
  75.5 0.0 copy-start.4
  75.5 0.1 convert_bitcast_fusion
  75.6 0.6 copy.15
  76.2 0.5 reshape.88
  76.7 0.0 copy-done.4
  76.8 0.9 %add_convert_fusion = bf16[2,8,14848]{2,1,0:T(8,128)(2,1)} fusion(f32[2,8,14848]{2,1,0:T(8,128)S(1)} %reshape.88, bf16[2,8,14848]{2,1,0:T(8,128)(2,1)S(1)} %copy-done.4), kind=kLoop, calls=%fused_computation.7 | loop fusion | flops 712704 | bytes 1900544 | tf_op jit(solution)/shard_map/convert_element_type | solution.py:352
  (7 shorter events, 0.1 us)
Async XLA Ops:
  0.0 37.9 %copy-start = (bf16[8,256,64]{1,2,0:T(8,128)(2,1)S(1)}, bf16[8,256,64]{1,2,0:T(8,128)(2,1)}, u32[]{:S(2)}) copy-start(bf16[8,256,64]{1,2,0:T(8,128)(2,1)} %param.10) | copy-start | bytes 786436
  2.5 2.1 %copy-start.2 = (bf16[928,1984]{1,0:T(8,128)(2,1)S(1)}, bf16[928,1984]{1,0:T(8,128)(2,1)}, u32[]{:S(2)}) copy-start(bf16[928,1984]{1,0:T(8,128)(2,1)} %w_hbm.2) | copy-start | bytes 11046916
  4.6 1.0 %copy-start.3 = (bf16[2,8,14848]{2,1,0:T(8,128)(2,1)S(1)}, bf16[2,8,14848]{2,1,0:T(8,128)(2,1)}, u32[]{:S(2)}) copy-start(bf16[2,8,14848]{2,1,0:T(8,128)(2,1)} %param.8) | copy-start | bytes 1425412
  5.6 33.1 %copy-start.5 = (bf16[8,256,64]{1,2,0:T(8,128)(2,1)S(1)}, bf16[8,256,64]{1,2,0:T(8,128)(2,1)}, u32[]{:S(2)}) copy-start(bf16[8,256,64]{1,2,0:T(8,128)(2,1)} %param.11) | copy-start | bytes 786436
  45.3 2.1 %copy-start.1 = (bf16[1856,928]{1,0:T(8,128)(2,1)S(1)}, bf16[1856,928]{1,0:T(8,128)(2,1)}, u32[]{:S(2)}) copy-start(bf16[1856,928]{1,0:T(8,128)(2,1)} %copy.14.w_hbm) | copy-start | bytes 10334212
  75.5 1.2 %copy-start.4 = (bf16[2,8,14848]{2,1,0:T(8,128)(2,1)S(1)}, bf16[2,8,14848]{2,1,0:T(8,128)(2,1)}, u32[]{:S(2)}) copy-start(bf16[2,8,14848]{2,1,0:T(8,128)(2,1)} %param.8) | copy-start | bytes 1425412

commit v3 on v2

--- a/solution.py
+++ b/solution.py
@@ -37,14 +37,13 @@
     return sorted(range(1, count), key=lambda k: abs(2 * k - count))
 
 
-def product(left, weights, store):
-    width = weights.shape[1]
+def product(left, weights, width, columns, store):
     for low in range(0, width, 512):
         high = min(low + 512, width)
+        block = weights[:, low:high] if columns else weights[low:high, :]
+        dims = (((1,), (1 - columns,)), ((), ()))
         store(
-            low,
-            high,
-            jnp.dot(left, weights[:, low:high], preferred_element_type=jnp.float32),
+            low, high, lax.dot_general(left, block, dims, preferred_element_type=jnp.float32)
         )
 
 
@@ -76,6 +75,10 @@
     chip = me // 2
     other = 1 - core
     sibling = chip * 2 + other
+    pairs = chips // 2
+    pair = chip // 2
+    side = lax.rem(chip, 2)
+    partner = (pair * 2 + 1 - side) * 2 + core
     part = w_ref.shape[0]
     rows, width = h_ref.shape
     far = far_first(count)
@@ -88,10 +91,12 @@
     centred = values - average
     variance = jnp.sum(centred * centred, axis=-1, keepdims=True) / width
     scale = lax.rsqrt(variance + 1e-05)
+    gain = gain_ref[...].reshape(1, width)
+    bias = bias_ref[...].reshape(1, width)
     for d in range(count):
         at = slice(d * part, (d + 1) * part)
         block = (h_ref[:, at].astype(jnp.float32) - average) * scale
-        normed[d] = (block * gain_ref[:, at] + bias_ref[:, at]).astype(jnp.bfloat16)
+        normed[d] = (block * gain[:, at] + bias[:, at]).astype(jnp.bfloat16)
     meet(everyone)
     copies = []
     for k in far:
@@ -110,30 +115,45 @@
         def store(low, high, tile):
             terms[which, :, :, low:high] = tile.reshape(chips, rows, high - low)
 
-        product(spread[which].reshape(chips * rows, part), w_ref, store)
+        product(spread[which].reshape(chips * rows, part), w_ref, w_ref.shape[1], 1, store)
 
     multiply(other)
-    order = far_first(chips)
+    order = far_first(pairs)
     firsts = {}
     for k in order + [0]:
-        j = lax.rem(chip + k, chips)
-        firsts[k] = remote(terms.at[other, j], sib.at[j], send_a.at[k], recv_a.at[k], sibling)
-        firsts[k].start()
+        for w in range(2):
+            j = lax.rem(pair + k, pairs) * 2 + (side if w else 1 - side)
+            sems = send_a.at[2 * k + w], recv_a.at[2 * k + w]
+            firsts[k, w] = remote(terms.at[other, j], sib.at[j], *sems, sibling)
+            firsts[k, w].start()
     multiply(core)
-    for k in order:
-        j = lax.rem(chip + k, chips)
-        firsts[k].wait_recv()
-        packed[j] = (terms[core, j] + sib[j]).astype(jnp.bfloat16)
-        copy = remote(packed.at[j], arrived.at[chip], send_b.at[k], recv_b.at[k], j * 2 + core)
+    for k in order + [0]:
+        to = lax.rem(pair + k, pairs)
+        j = to * 2 + 1 - side
+        firsts[k, 0].wait_recv()
+        packed[0, to] = (terms[core, j] + sib[j]).astype(jnp.bfloat16)
+        copy = remote(packed.at[0, to], arrived.at[0, to], send_b.at[k], recv_b.at[k], partner)
         copy.start()
         copies.append(copy)
-    firsts[0].wait_recv()
-    total = terms[core, chip] + sib[chip]
+    for k in order + [0]:
+        to = lax.rem(pair + k, pairs)
+        j = to * 2 + side
+        firsts[k, 1].wait_recv()
+        block = arrived.at[0, to]
+        remote(block, block, send_b.at[k], recv_b.at[k], partner).wait_recv()
+        total = terms[core, j] + sib[j] + arrived[0, to].astype(jnp.float32)
+        if k:
+            packed[1, to] = total.astype(jnp.bfloat16)
+            sems = send_b.at[pairs + k], recv_b.at[pairs + k]
+            copy = remote(packed.at[1, to], arrived.at[1, pair], *sems, j * 2 + core)
+            copy.start()
+            copies.append(copy)
     for k in order[::-1]:
-        sender = lax.rem(chip + chips - k, chips)
-        block = arrived.at[sender]
-        remote(block, block, send_b.at[k], recv_b.at[k], sender * 2 + core).wait_recv()
-        total = total + arrived[sender].astype(jnp.float32)
+        sender = lax.rem(pair + pairs - k, pairs)
+        block = arrived.at[1, sender]
+        sems = send_b.at[pairs + k], recv_b.at[pairs + k]
+        remote(block, block, *sems, (sender * 2 + side) * 2 + core).wait_recv()
+        total = total + arrived[1, sender].astype(jnp.float32)
     o_ref[...] = total.astype(jnp.bfloat16)
     for copy in list(firsts.values()) + copies:
         copy.wait_send()
@@ -147,7 +167,7 @@
         out_specs=pl.BlockSpec(memory_space=VMEM),
         scratch_shapes=scratch,
         compiler_params=pltpu.CompilerParams(
-            collective_id=collective_id, has_side_effects=True, vmem_limit_bytes=48 * 2**20
+            collective_id=collective_id, has_side_effects=True, vmem_limit_bytes=60 * 2**20
         ),
     )(*args)
 
@@ -167,8 +187,8 @@
             VMEM((2, chips, rows, part), half),
             VMEM((2, chips, rows, width), jnp.float32),
             VMEM((chips, rows, width), jnp.float32),
-            VMEM((chips, rows, width), half),
-            VMEM((chips, rows, width), half),
+            VMEM((2, chips // 2, rows, width), half),
+            VMEM((2, chips // 2, rows, width), half),
             DMA,
         ]
         + [DMA((count,))] * 2
@@ -184,11 +204,13 @@
 def output_kernel(
     count,
     m_ref,
+    h_ref,
     w_hbm,
     o_ref,
     w_ref,
     heads,
     columns,
+    landed,
     w_sem,
     send_a,
     recv_a,
@@ -252,15 +274,15 @@
                 chips, rows, high - low
             )
 
-        product(heads[which].reshape(chips * rows, depth), w_ref, store)
+        product(heads[which].reshape(chips * rows, depth), w_ref, w_ref.shape[0], 0, store)
 
     spans = far_first(chips)
     multiply(core)
     for k in spans:
         j = lax.rem(chip + k, chips)
         sems = send_x.at[k], recv_x.at[k]
-        push(remote(columns.at[core, j], o_ref.at[me], *sems, j * 2 + core))
-    o_ref[me] = columns[core, chip]
+        push(remote(columns.at[core, j], landed.at[me], *sems, j * 2 + core))
+    landed[me] = columns[core, chip]
     for far in range(2):
         for k in [0] + order:
             source = lax.rem(pair + pairs - k, pairs) * 2 + (1 - side if far else side)
@@ -271,32 +293,39 @@
     for k in spans + [0]:
         j = lax.rem(chip + k, chips)
         sems = send_x.at[chips + k], recv_x.at[chips + k]
-        push(remote(columns.at[other, j], o_ref.at[me], *sems, j * 2 + other))
+        push(remote(columns.at[other, j], landed.at[me], *sems, j * 2 + other))
     for k in spans:
         sender = lax.rem(chip + chips - k, chips) * 2 + core
-        block = o_ref.at[sender]
+        block = landed.at[sender]
         remote(block, block, send_x.at[k], recv_x.at[k], sender).wait_recv()
     for k in spans + [0]:
         sender = lax.rem(chip + chips - k, chips) * 2 + other
-        block = o_ref.at[sender]
+        block = landed.at[sender]
         remote(block, block, send_x.at[chips + k], recv_x.at[chips + k], sender).wait_recv()
+    part = landed.shape[2]
+    for d in range(count):
+        at = slice(d * part, (d + 1) * part)
+        moved = h_ref[:, at].astype(jnp.float32) + landed[d].astype(jnp.float32)
+        o_ref[:, at] = moved.astype(jnp.bfloat16)
     for copy in copies:
         copy.wait_send()
 
 
-def output(mixed, w_out, count, collective_id):
+def output(mixed, hidden, w_out, count, collective_id):
     rows, depth = mixed.shape
     part = w_out.shape[1]
+    turned = w_out.T
     chips = count // 2
     half = jnp.bfloat16
     return call(
         functools.partial(output_kernel, count),
-        jax.ShapeDtypeStruct((count, rows, part), half),
-        [VMEM, pl.ANY],
+        jax.ShapeDtypeStruct(hidden.shape, half),
+        [VMEM, VMEM, pl.ANY],
         [
-            VMEM((depth, part), half),
+            VMEM((part, depth), half),
             VMEM((2, chips, rows, depth), half),
             VMEM((2, chips, rows, part), half),
+            VMEM((count, rows, part), half),
             DMA,
         ]
         + [DMA((chips // 2,))] * 4
@@ -304,7 +333,8 @@
         + [DMA((count,))] * 2,
         collective_id,
         mixed,
-        w_out,
+        hidden,
+        turned,
     )
 
 
@@ -339,7 +369,7 @@
     count = lax.axis_size("loop")
     both = steps * rows
     projected = project(
-        hidden.reshape(both, width), ln_gain[None], ln_bias[None], w_qkv, count, 0
+        hidden.reshape(both, width), ln_gain, ln_bias, w_qkv, count, 0
     )
     projected = projected.reshape(steps, rows, -1).transpose(1, 0, 2)
     queries = projected[:, :, : heads * head_dim].reshape(rows, steps, heads, head_dim)
@@ -347,9 +377,8 @@
     fresh_values = projected[:, :, (heads + 1) * head_dim :]
     mixed = attend(queries, fresh_keys, fresh_values, cache_keys, cache_values, lengths)
     mixed = mixed.transpose(1, 0, 2).reshape(steps * rows, -1)
-    attention = output(mixed, w_out, count, 1)
-    attention = attention.transpose(1, 0, 2).reshape(steps, rows, width)
-    return (hidden.astype(jnp.float32) + attention.astype(jnp.float32)).astype(jnp.bfloat16)
+    moved = output(mixed, hidden.reshape(both, width), w_out, count, 1)
+    return moved.reshape(steps, rows, width)
 
 
 def solution(mesh):

time: 78.1 us -> 68.7 us (0.88)
  local copies, waits for them, and re-layouts: 14.5 us -> 3.72 us
  Pallas kernels: 59.8 us -> 62.5 us
  other arithmetic: 2.06 us -> 1.11 us
    unnamed x13 -> x5, local copies, waits for them, and re-layouts: 11.2 us -> 1.84 us
    pallas_call x2, Pallas kernels: 59.8 us -> 62.5 us  [call(): pl.pallas_call(kernel, out_shape=out, in_specs=[pl.BlockSpec(memory_space...]
    broadcast_in_dim x2 -> x0, local copies, waits for them, and re-layouts: 1.74 us -> none  [the longest x1 0.87 us: local(): ln_bias[None]]
    convert_element_type x2 -> x0, local copies, waits for them, and re-layouts: 1.1 us -> none  [local(): attention.astype(jnp.float32)]
    convert_element_type x2 -> x0, other arithmetic: 0.96 us -> none  [the longest x1 0.85 us: local(): (hidden.astype(jnp.float32) + attention.astype(jnp.float32)).astype(jnp.b...]
    reshape x1, local copies, waits for them, and re-layouts: 0.07 us -> 0.91 us  [local(): projected = projected.reshape(steps, rows, -1).transpose(1, 0, 2)]
where the time goes in v3:
time: 68.7 us; the launch traced here: 68.5 us
  Pallas kernels  62.5 us (91%)
  local copies, waits for them, and re-layouts  3.72 us (5%)
  other arithmetic  1.11 us (2%)
  matrix products  1.09 us (2%)
    pallas_call x2, Pallas kernels, call(): pl.pallas_call(kernel, out_shape=out, in_specs=[pl.BlockSpec(memory_space...  62.5 us
    unnamed x5, local copies, waits for them, and re-layouts  1.84 us

profile of v3, /device:TPU:1, one launch (start us, length us, event | category | flops | bytes accessed | tf_op | source)
XLA Modules:
  0.0 68.5 jit_solution(18418544541040126023)
XLA Ops:
  0.0 0.0 copy-start
  0.0 0.0 copy-start.1
  0.0 0.8 %iota_compare_fusion = pred[8,256]{1,0:T(8,128)(4,1)S(1)} fusion(s32[8]{0:T(128)} %param.9), kind=kLoop, calls=%fused_computation.14 | loop fusion | flops 2048 | bytes 2080 | tf_op jit(solution)/shard_map/lt | solution.py:345
  0.8 30.6 %shard_map.82 = bf16[16,1984]{1,0:T(8,128)(2,1)} custom-call(bf16[16,14848]{1,0:T(8,128)(2,1)} %bitcast.17, f32[14848]{0:T(1024)} %gain_ref.1, f32[14848]{0:T(1024)} %bias_ref.1, bf16[928,1984]{1,0:T(8,128)(2,1)} %w_hbm.1), custom_call_target="tpu_custom_call" | custom-call | tf_op jit(solution)/shard_map/pallas_call | solution.py:163
  31.4 0.9 %copy.15 = bf16[2,8,1984]{2,0,1:T(2,128)(2,1)S(1)} copy(bf16[2,8,1984]{2,1,0:T(8,128)(2,1)} %bitcast.19) | data formatting | bytes 126976 | tf_op jit(solution)/shard_map/reshape | solution.py:374
  32.4 0.1 reshape_reshape.3
  32.5 0.2 fusion.13
  32.8 0.0 copy-done
  32.8 0.3 fusion.12
  33.1 0.3 fusion.3
  33.4 0.2 fusion.7
  33.7 0.0 copy-done.1
  33.7 0.3 fusion.1
  34.0 0.1 convert_element_type.15
  34.2 0.6 copy.16
  34.8 31.8 %shard_map.83 = bf16[16,14848]{1,0:T(8,128)(2,1)} custom-call(bf16[16,1856]{1,0:T(8,128)(2,1)} %bitcast.24, bf16[16,14848]{1,0:T(8,128)(2,1)} %bitcast.18, bf16[928,1856]{1,0:T(8,128)(2,1)} %bitcast.15), custom_call_target="tpu_custom_call" | custom-call | tf_op jit(solution)/shard_map/pallas_call | solution.py:163
  66.6 1.8 %copy.18 = bf16[2,8,14848]{2,1,0:T(8,128)(2,1)} copy(bf16[2,8,14848]{2,1,0:T(8,128)(2,1)} %bitcast.16) | data formatting | bytes 950272
  (6 shorter events, 0.1 us)
Async XLA Ops:
  0.0 32.8 %copy-start = (bf16[8,256,64]{1,2,0:T(8,128)(2,1)S(1)}, bf16[8,256,64]{1,2,0:T(8,128)(2,1)}, u32[]{:S(2)}) copy-start(bf16[8,256,64]{1,2,0:T(8,128)(2,1)} %param.10) | copy-start | bytes 786436
  0.0 33.7 %copy-start.1 = (bf16[8,256,64]{1,2,0:T(8,128)(2,1)S(1)}, bf16[8,256,64]{1,2,0:T(8,128)(2,1)}, u32[]{:S(2)}) copy-start(bf16[8,256,64]{1,2,0:T(8,128)(2,1)} %param.11) | copy-start | bytes 786436
